TPU v7x, 512 devices: a whole 4x8x8 slice. The times are simulated.
512 devices in a mesh: led: 8 (over z_hi, core), row: 64 (over y, x, z_lo).
Axes of the slice: x: 4, y: 8, z: 8 (z_hi: 4, z_lo: 2; z = z_hi * 2 + z_lo), core: 2. Of those that a mesh axis runs over, the one named last changes fastest.
Arguments:
- fields: float32 [2, 16, 2, 1024, 1024], P(None, 'led', None, 'row'), may hold values from -6 to 6
- phases: float32 [2, 1024, 1024], P(None, 'row'), may hold values from -3.140625 to 3.140625
- residual: float32 [16, 2, 1024, 1024], P('led', None, 'row'), may hold values from -6 to 6
- led_index: int32 [16], P('led'), may hold values from 0 to 224
Outputs:
- slopes: float32 [2, 1024, 1024], P(None, 'row', 'led')
- adjoint_wave: float32 [16, 2, 1024, 1024], P('led', None, 'row')
All inputs are finite; a program needn't handle non-finite values.
Results may differ from a plain program's by a relative error of at most 0.0003.
Values sent between devices are 32-bit elements; how exact they have to be, the bound alone decides.
A program may use at most 64 MiB of HBM per device.

v0:
```python
import math

import jax
import jax.numpy as jnp
import numpy as np
from jax import lax
from jax.experimental import pallas as pl
from jax.experimental.pallas import tpu as pltpu
from jax.sharding import PartitionSpec as P

N = 1024
GRID = 15
DZ = 64
SHIFT = 10
LANES = 128
TILE = 8
VMEM_LIMIT = 58 * 1024 * 1024
ROWS = 16
PEERS = 64
GROUPS = 8
LEDS = 2
SLICES = 2
MESH = pl.DeviceIdType.MESH
F32 = jnp.float32
BF16 = jnp.bfloat16


def dft_block(length):
    index = np.arange(length)
    angle = 2.0 * np.pi * (np.outer(index, index) % length) / length
    return np.cos(angle), np.sin(angle)


def complex_left(length):
    cos, sin = dft_block(length)
    return np.block([[cos, sin], [-sin, cos]])


def tables():
    wide = complex_left(LANES).astype(np.float32)
    long = complex_left(PEERS).astype(np.float32)
    cos, sin = dft_block(ROWS)
    eye = np.eye(LANES // ROWS)
    cos, sin = np.kron(eye, cos), np.kron(eye, sin)
    short = np.block([[cos, -sin], [sin, cos]]).astype(np.float32)
    angle = 2.0 * np.pi * np.outer(np.arange(TILE), np.arange(LANES)) / N
    turn_rows = np.concatenate([np.cos(angle), np.sin(angle)]).astype(np.float32)
    angle = 2.0 * np.pi * np.outer(np.arange(PEERS), np.arange(LANES) % ROWS) / N
    turn_cols = np.stack([np.cos(angle), np.sin(angle)]).astype(np.float32)
    return wide, long, short, turn_rows, turn_cols


def fit_turns():
    nodes = 0.5 * np.cos(np.pi * (np.arange(400) + 0.5) / 800)
    square = nodes * nodes
    basis = np.vander(square, 8, increasing=True)
    sin_fit = np.linalg.lstsq(basis, np.sin(2 * np.pi * nodes) / nodes, rcond=None)[0]
    cos_fit = np.linalg.lstsq(basis, np.cos(2 * np.pi * nodes), rcond=None)[0]
    return [float(v) for v in sin_fit], [float(v) for v in cos_fit]


SIN_FIT, COS_FIT = fit_turns()


def cos_sin_turns(turns):
    frac = turns - jnp.floor(turns + 0.5)
    square = frac * frac
    sine = jnp.full_like(square, SIN_FIT[-1])
    cosine = jnp.full_like(square, COS_FIT[-1])
    for s, c in zip(SIN_FIT[-2::-1], COS_FIT[-2::-1]):
        sine = sine * square + s
        cosine = cosine * square + c
    return cosine, sine * frac


def split(value):
    high = value.astype(BF16)
    return high, (value - high.astype(F32)).astype(BF16)


def dot3(left, right, dims):
    def dot(a, b):
        return lax.dot_general(a, b, (dims, ((), ())), preferred_element_type=F32)

    return dot(left[0], right[0]) + (dot(left[0], right[1]) + dot(left[1], right[0]))


def radix8(real, imag):
    half = math.sqrt(0.5)

    def pair(a, b):
        return (a[0] + b[0], a[1] + b[1]), (a[0] - b[0], a[1] - b[1])

    def minus_i(a):
        return a[1], -a[0]

    def four(z):
        s0, d0 = pair(z[0], z[2])
        s1, d1 = pair(z[1], z[3])
        y0, y2 = pair(s0, s1)
        y1, y3 = pair(d0, minus_i(d1))
        return [y0, y1, y2, y3]

    z = list(zip(real, imag))
    even = four([z[0], z[2], z[4], z[6]])
    odd = four([z[1], z[3], z[5], z[7]])
    odd[1] = ((odd[1][0] + odd[1][1]) * half, (odd[1][1] - odd[1][0]) * half)
    odd[2] = minus_i(odd[2])
    odd[3] = ((odd[3][1] - odd[3][0]) * half, (odd[3][0] + odd[3][1]) * -half)
    out = [None] * 8
    for k in range(4):
        out[k], out[k + 4] = pair(even[k], odd[k])
    return [o[0] for o in out], [o[1] for o in out]


def twist(real, imag, cos, sin):
    return real * cos + imag * sin, imag * cos - real * sin


def row_forward(real, imag, turn_cos, turn_sin, wide):
    real, imag = radix8(real, imag)
    rows = []
    for k in range(8):
        re, im = (real[k], imag[k]) if k == 0 else twist(real[k], imag[k], turn_cos[k], turn_sin[k])
        rows.append(jnp.concatenate([re, im], axis=1))
    return dot3(wide, split(jnp.concatenate(rows, axis=0)), ((1,), (1,)))


def row_inverse(swapped, turn_cos, turn_sin, wide):
    spread = dot3(wide, split(swapped), ((1,), (0,)))
    first = spread[:LANES].T
    second = spread[LANES:].T
    real, imag = [], []
    for k in range(8):
        re, im = first[ROWS * k : ROWS * (k + 1)], second[ROWS * k : ROWS * (k + 1)]
        if k > 0:
            re, im = twist(re, im, turn_cos[k], turn_sin[k])
        real.append(re)
        imag.append(im)
    return radix8(real, imag)


def column_forward(blocks, turn_cos, turn_sin, long, short):
    stacked = jnp.concatenate([jnp.concatenate(blocks[c], axis=1) for c in range(2)], axis=0)
    mixed = dot3(long, split(stacked), ((1,), (0,)))
    rows = []
    for k in range(2):
        re = mixed[:PEERS, LANES * k : LANES * (k + 1)]
        im = mixed[PEERS:, LANES * k : LANES * (k + 1)]
        rows.append(jnp.concatenate(twist(re, im, turn_cos, turn_sin), axis=1))
    return dot3(split(jnp.concatenate(rows, axis=0)), short, ((1,), (0,)))


def column_inverse(real, imag, turn_cos, turn_sin, long, short):
    mixed = dot3(split(jnp.concatenate([real, imag], axis=1)), short, ((1,), (0,)))
    first, second = [], []
    for k in range(2):
        block = mixed[PEERS * k : PEERS * (k + 1)]
        re, im = twist(block[:, :LANES], block[:, LANES:], turn_cos, turn_sin)
        first.append(re)
        second.append(im)
    stacked = jnp.concatenate(
        [jnp.concatenate(first, axis=1), jnp.concatenate(second, axis=1)], axis=0
    )
    return dot3(long, split(stacked), ((1,), (0,)))


def filter_block(owner, k2lo, led):
    lane = lax.broadcasted_iota(jnp.int32, (PEERS, LANES), 1)
    v1 = lax.broadcasted_iota(jnp.int32, (PEERS, LANES), 0)
    u = (lane >> 4) + 8 * (PEERS * k2lo + owner)
    v = v1 + PEERS * (lane & (ROWS - 1))
    kx = (led // GRID - GRID // 2) * SHIFT
    ky = (led % GRID - GRID // 2) * SHIFT
    fx = (((u + N // 2) & (N - 1)) - N // 2 + kx).astype(F32) * (1.0 / N)
    fy = (((v + N // 2) & (N - 1)) - N // 2 + ky).astype(F32) * (1.0 / N)
    turns = DZ * (jnp.sqrt(1.0 - fx * fx - fy * fy) - 1.0)
    cosine, sine = cos_sin_turns(turns)
    return cosine * (1.0 / (N * N)), sine * (1.0 / (N * N))


def kernel(
    led_ref, fields_hbm, phases_hbm, residual_hbm, wide_hbm, long_hbm, short_hbm, trow_hbm, tcol_hbm,
    slopes_hbm, wave_hbm,
    fields, phases, wave, wide_f32, long_f32, short_f32, trow, tcol, wide_ref, long_ref, short_ref,
    filt, trans, out_box, in_box, slope_out, slope_in, slopes,
    load_sem, send_sem, recv_sem, lsend_sem, lrecv_sem, store_sem,
):
    me = lax.axis_index("row")
    group = lax.axis_index("led")
    my_y, my_w = me // 8, me % 8
    led_peers = [lax.rem(group + d, GROUPS) for d in (4, 3, 5, 2, 6, 7, 1)]

    loads = [
        pltpu.make_async_copy(src, dst, load_sem.at[n])
        for n, (src, dst) in enumerate(
            [
                (residual_hbm, wave),
                (trow_hbm, trow),
                (wide_hbm, wide_f32),
                (tcol_hbm, tcol),
                (long_hbm, long_f32),
                (short_hbm, short_f32),
                (phases_hbm, phases),
                (fields_hbm, fields),
            ]
        )
    ]
    for load in loads:
        load.start()

    barrier = pltpu.get_barrier_semaphore()

    @pl.loop(1, PEERS)
    def _(step):
        peer = lax.rem(me + step, PEERS)
        pl.semaphore_signal(barrier, inc=1, device_id=(group, peer), device_id_type=MESH)

    for peer in led_peers:
        pl.semaphore_signal(barrier, inc=1, device_id=(peer, me), device_id_type=MESH)

    for load in loads[:3]:
        load.wait()
    turn_cos = [trow[k : k + 1, :] for k in range(8)]
    turn_sin = [trow[8 + k : 9 + k, :] for k in range(8)]
    wide_ref[0], wide_ref[1] = split(wide_f32[...])

    def halves(table):
        return table[0], table[1]

    bases = [lax.rem(my_y + dy, 8) * 8 for dy in range(8)]

    def send_tile(slot, peer):
        pltpu.make_async_remote_copy(
            src_ref=out_box.at[slot, peer],
            dst_ref=in_box.at[slot, me],
            send_sem=send_sem.at[slot],
            recv_sem=recv_sem.at[slot],
            device_id=(group, peer),
            device_id_type=MESH,
        ).start()

    def send(slot):
        @pl.loop(1, 8)
        def _(dw):
            column = lax.rem(my_w + dw, 8)
            for dy in (4, 3, 5, 2, 6, 1, 7, 0):
                send_tile(slot, bases[dy] + column)

        for dy in (4, 3, 5, 2, 6, 1, 7):
            send_tile(slot, bases[dy] + my_w)
        pltpu.make_async_copy(out_box.at[slot, me], in_box.at[slot, me], recv_sem.at[slot]).start()

    def put(values, slot):
        flat = out_box.at[slot].reshape(PEERS * 4, LANES)
        for j in range(4):
            flat[pl.ds(j, PEERS, stride=4), :] = values[j]

    def arrived(slot):
        whole = in_box.at[slot]
        pltpu.make_async_copy(whole, whole, recv_sem.at[slot]).wait()
        flat = whole.reshape(PEERS * 4, LANES)
        return [flat[pl.ds(j, PEERS, stride=4), :] for j in range(4)]

    def columns_of(ref, c):
        return [ref[c, :, LANES * a : LANES * (a + 1)] for a in range(8)]

    def to_columns(led, slot):
        seed = wave.at[led]
        spectrum = row_forward(
            columns_of(seed, 0), columns_of(seed, 1), turn_cos, turn_sin, halves(wide_ref)
        )
        put([spectrum[PEERS * j : PEERS * (j + 1)] for j in range(4)], slot)

    def slot_of(turn, way, led):
        return (2 * turn + way) * LEDS + led

    def column_pass(turn, led):
        tiles = arrived(slot_of(turn, 0, led))
        spectrum = column_forward([tiles[:2], tiles[2:]], tcol[0], tcol[1], halves(long_ref), halves(short_ref))
        real, imag = twist(spectrum[:, :LANES], spectrum[:, LANES:], filt[led, 0], filt[led, 1])
        back = column_inverse(imag, real, tcol[0], tcol[1], halves(long_ref), halves(short_ref))
        values = [
            back[PEERS * (1 - c) : PEERS * (2 - c), LANES * k : LANES * (k + 1)]
            for c in range(2)
            for k in range(2)
        ]
        put(values, slot_of(turn, 1, led))
        send(slot_of(turn, 1, led))

    def send_slopes(turn):
        for peer in led_peers:
            pltpu.make_async_remote_copy(
                src_ref=slope_out.at[turn, peer],
                dst_ref=slope_in.at[turn, group],
                send_sem=lsend_sem.at[turn],
                recv_sem=lrecv_sem.at[turn],
                device_id=(peer, me),
                device_id_type=MESH,
            ).start()
        pltpu.make_async_copy(
            slope_out.at[turn, group], slope_in.at[turn, group], lrecv_sem.at[turn]
        ).start()

    def from_columns(turn, led):
        layer = SLICES - 1 - turn
        tiles = arrived(slot_of(turn, 1, led))
        swapped = jnp.concatenate([tiles[2], tiles[3], tiles[0], tiles[1]], axis=0)
        imag, real = row_inverse(swapped, turn_cos, turn_sin, halves(wide_ref))
        for a in range(8):
            cols = slice(LANES * a, LANES * (a + 1))
            re, im = twist(real[a], imag[a], trans[layer, 0, :, cols], trans[layer, 1, :, cols])
            wave[led, 0, :, cols] = re
            wave[led, 1, :, cols] = im

    def slope_terms(turn, led):
        layer = SLICES - 1 - turn
        for a in range(8):
            cols = slice(LANES * a, LANES * (a + 1))
            slope_out[turn, a] += (
                fields[layer, led, 0, :, cols] * wave[led, 1, :, cols]
                - fields[layer, led, 1, :, cols] * wave[led, 0, :, cols]
            )

    slope_out[...] = jnp.zeros_like(slope_out)

    @pl.loop(0, SLICES + 1)
    def _(phase):
        @pl.loop(0, LEDS)
        def _(led):
            @pl.when(phase > 0)
            def _():
                from_columns(phase - 1, led)

            @pl.when(phase < SLICES)
            def _():
                to_columns(led, slot_of(phase, 0, led))

                @pl.when(phase + led == 0)
                def _():
                    pl.semaphore_wait(barrier, PEERS - 1 + GROUPS - 1)

                send(slot_of(phase, 0, led))

            @pl.when(phase > 0)
            def _():
                slope_terms(phase - 1, led)

                @pl.when(led == LEDS - 1)
                def _():
                    send_slopes(phase - 1)

            @pl.when(phase == SLICES)
            def _():
                pltpu.make_async_copy(wave.at[led], wave_hbm.at[led], store_sem.at[led]).start()

        @pl.when(phase == 0)
        def _():
            for led in range(LEDS):
                for k in range(2):
                    cosine, sine = filter_block(me, k, led_ref[led])
                    filt[led, 0, PEERS * k : PEERS * (k + 1), :] = cosine
                    filt[led, 1, PEERS * k : PEERS * (k + 1), :] = sine
            for load in loads[3:]:
                load.wait()
            long_ref[0], long_ref[1] = split(long_f32[...])
            short_ref[0], short_ref[1] = split(short_f32[...])
            for layer in range(SLICES):
                cosine, sine = cos_sin_turns(phases[layer] * (0.5 / math.pi))
                trans[layer, 0] = cosine
                trans[layer, 1] = sine

        @pl.when(phase < SLICES)
        def _():
            @pl.loop(0, LEDS)
            def _(led):
                column_pass(phase, led)

    for turn in range(SLICES):
        pltpu.make_async_copy(slope_in.at[turn], slope_in.at[turn], lrecv_sem.at[turn]).wait()
        slopes[SLICES - 1 - turn] = jnp.sum(slope_in[turn], axis=0) * (1.0 / (LEDS * GROUPS))
    store_slopes = pltpu.make_async_copy(slopes, slopes_hbm, store_sem.at[LEDS])
    store_slopes.start()
    for slot in range(2 * SLICES * LEDS):
        sent = out_box.at[slot, pl.ds(0, PEERS - 1)]
        pltpu.make_async_copy(sent, sent, send_sem.at[slot]).wait()
    for turn in range(SLICES):
        sent = slope_out.at[turn, pl.ds(0, GROUPS - 1)]
        pltpu.make_async_copy(sent, sent, lsend_sem.at[turn]).wait()
    for led in range(LEDS):
        pltpu.make_async_copy(wave.at[led], wave_hbm.at[led], store_sem.at[led]).wait()
    store_slopes.wait()


def local(fields, phases, residual, led_index):
    consts = [jnp.asarray(t) for t in tables()]
    scratch = [
        pltpu.VMEM(fields.shape, F32),
        pltpu.VMEM(phases.shape, F32),
        pltpu.VMEM(residual.shape, F32),
    ]
    slots = 2 * SLICES * LEDS
    scratch += [pltpu.VMEM(t.shape, t.dtype) for t in consts]
    scratch += [pltpu.VMEM((2,) + t.shape, BF16) for t in consts[:3]]
    scratch += [
        pltpu.VMEM((LEDS, 2, LANES, LANES), F32),
        pltpu.VMEM((SLICES, 2, ROWS, N), F32),
    ]
    scratch += [pltpu.VMEM((slots, PEERS, 4, LANES), F32)] * 2
    scratch += [
        pltpu.VMEM((SLICES, GROUPS, ROWS, LANES), F32),
        pltpu.VMEM((SLICES, GROUPS, ROWS, LANES), F32),
        pltpu.VMEM((SLICES, ROWS, LANES), F32),
        pltpu.SemaphoreType.DMA((8,)),
        pltpu.SemaphoreType.DMA((slots,)),
        pltpu.SemaphoreType.DMA((slots,)),
        pltpu.SemaphoreType.DMA((SLICES,)),
        pltpu.SemaphoreType.DMA((SLICES,)),
        pltpu.SemaphoreType.DMA((LEDS + 1,)),
    ]
    anywhere = pl.BlockSpec(memory_space=pl.ANY)
    return pl.pallas_call(
        kernel,
        out_shape=(
            jax.ShapeDtypeStruct((SLICES, ROWS, LANES), F32),
            jax.ShapeDtypeStruct(residual.shape, F32),
        ),
        in_specs=[pl.BlockSpec(memory_space=pltpu.SMEM)] + [anywhere] * 8,
        out_specs=(anywhere, anywhere),
        scratch_shapes=scratch,
        compiler_params=pltpu.CompilerParams(
            collective_id=0, has_side_effects=True, vmem_limit_bytes=VMEM_LIMIT
        ),
        name="adjoint",
    )(led_index, fields, phases, residual, *consts)


def solution(mesh):
    in_specs = (
        P(None, "led", None, "row", None),
        P(None, "row", None),
        P("led", None, "row", None),
        P("led"),
    )
    out_specs = (P(None, "row", "led"), P("led", None, "row", None))
    return jax.shard_map(local, mesh=mesh, in_specs=in_specs, out_specs=out_specs, check_vma=False)
```

profile of v0, /device:TPU:1, one launch (start us, length us, event | category | flops | bytes accessed | tf_op | source)
XLA Modules:
  0.0 61.9 jit_solution(3642137946013913767)
XLA Ops:
  0.6 58.3 %adjoint.1 = (f32[2,16,128]{2,1,0:T(8,128)}, f32[2,2,16,1024]{3,2,1,0:T(8,128)}) custom-call(s32[2]{0:T(128)} %led_ref.1, f32[2,2,2,16,1024]{4,3,2,1,0:T(8,128)} %fields_hbm.1, f32[2,16,1024]{2,1,0:T(8,128)} %phases_hbm.1, f32[2,2,16,1024]{3,2,1,0:T(8,128)} %residual_hbm.1, f32[256,256]{1,0:T(8,128)} %constant.10.clone.wide_hbm, ...), custom_call_target="tpu_custom_call" | custom-call | tf_op jit(solution)/shard_map/adjoint/pallas_call | solution.py:422
  58.9 1.3 %copy.13 = f32[2,16,128]{2,1,0:T(8,128)} copy(f32[2,16,128]{2,1,0:T(8,128)} %get-tuple-element.4) | data formatting | bytes 32768
  60.2 1.7 %copy.14 = f32[2,2,16,1024]{3,2,1,0:T(8,128)} copy(f32[2,2,16,1024]{3,2,1,0:T(8,128)} %get-tuple-element.5) | data formatting | bytes 524288
where the time goes:
time: 62.1 us; the launch traced here: 61.9 us
  Pallas kernels  58.3 us (94%)
  local copies, waits for them, and re-layouts  2.99 us (5%)
  between operations  0.64 us (1%)
    pallas_call x1, Pallas kernels, local(): pl.pallas_call(kernel, out_shape=(jax.ShapeDtypeStruct((SLICES, ROWS, LAN...  58.3 us
    unnamed x2, local copies, waits for them, and re-layouts  2.99 us

commit v1 on v0

--- a/solution.py
+++ b/solution.py
@@ -14,7 +14,7 @@
 SHIFT = 10
 LANES = 128
 TILE = 8
-VMEM_LIMIT = 58 * 1024 * 1024
+VMEM_LIMIT = 40 * 1024 * 1024
 ROWS = 16
 PEERS = 64
 GROUPS = 8
@@ -180,11 +180,11 @@
 
 
 def kernel(
-    led_ref, fields_hbm, phases_hbm, residual_hbm, wide_hbm, long_hbm, short_hbm, trow_hbm, tcol_hbm,
-    slopes_hbm, wave_hbm,
-    fields, phases, wave, wide_f32, long_f32, short_f32, trow, tcol, wide_ref, long_ref, short_ref,
-    filt, trans, out_box, in_box, slope_out, slope_in, slopes,
-    load_sem, send_sem, recv_sem, lsend_sem, lrecv_sem, store_sem,
+    led_hbm, fields_hbm, phases_hbm, residual_hbm, wide_hbm, long_hbm, short_hbm, trow_hbm, tcol_hbm,
+    slopes, wave,
+    led_ref, fields, phases, wide_f32, long_f32, short_f32, trow, tcol, wide_ref, long_ref, short_ref,
+    filt, trans, out_box, in_box, slope_out, slope_in,
+    load_sem, send_sem, recv_sem, lsend_sem, lrecv_sem,
 ):
     me = lax.axis_index("row")
     group = lax.axis_index("led")
@@ -203,6 +203,7 @@
                 (short_hbm, short_f32),
                 (phases_hbm, phases),
                 (fields_hbm, fields),
+                (led_hbm, led_ref),
             ]
         )
     ]
@@ -240,15 +241,13 @@
             device_id_type=MESH,
         ).start()
 
+    columns = [lax.rem(my_w + dw, 8) for dw in range(8)]
+
     def send(slot):
-        @pl.loop(1, 8)
-        def _(dw):
-            column = lax.rem(my_w + dw, 8)
+        for dw in (5, 4, 3, 1, 7, 2, 6, 0):
             for dy in (4, 3, 5, 2, 6, 1, 7, 0):
-                send_tile(slot, bases[dy] + column)
-
-        for dy in (4, 3, 5, 2, 6, 1, 7):
-            send_tile(slot, bases[dy] + my_w)
+                if dw + dy > 0:
+                    send_tile(slot, bases[dy] + columns[dw])
         pltpu.make_async_copy(out_box.at[slot, me], in_box.at[slot, me], recv_sem.at[slot]).start()
 
     def put(values, slot):
@@ -350,19 +349,15 @@
                 def _():
                     send_slopes(phase - 1)
 
-            @pl.when(phase == SLICES)
-            def _():
-                pltpu.make_async_copy(wave.at[led], wave_hbm.at[led], store_sem.at[led]).start()
-
         @pl.when(phase == 0)
         def _():
+            for load in loads[3:]:
+                load.wait()
             for led in range(LEDS):
                 for k in range(2):
                     cosine, sine = filter_block(me, k, led_ref[led])
                     filt[led, 0, PEERS * k : PEERS * (k + 1), :] = cosine
                     filt[led, 1, PEERS * k : PEERS * (k + 1), :] = sine
-            for load in loads[3:]:
-                load.wait()
             long_ref[0], long_ref[1] = split(long_f32[...])
             short_ref[0], short_ref[1] = split(short_f32[...])
             for layer in range(SLICES):
@@ -379,25 +374,20 @@
     for turn in range(SLICES):
         pltpu.make_async_copy(slope_in.at[turn], slope_in.at[turn], lrecv_sem.at[turn]).wait()
         slopes[SLICES - 1 - turn] = jnp.sum(slope_in[turn], axis=0) * (1.0 / (LEDS * GROUPS))
-    store_slopes = pltpu.make_async_copy(slopes, slopes_hbm, store_sem.at[LEDS])
-    store_slopes.start()
     for slot in range(2 * SLICES * LEDS):
         sent = out_box.at[slot, pl.ds(0, PEERS - 1)]
         pltpu.make_async_copy(sent, sent, send_sem.at[slot]).wait()
     for turn in range(SLICES):
         sent = slope_out.at[turn, pl.ds(0, GROUPS - 1)]
         pltpu.make_async_copy(sent, sent, lsend_sem.at[turn]).wait()
-    for led in range(LEDS):
-        pltpu.make_async_copy(wave.at[led], wave_hbm.at[led], store_sem.at[led]).wait()
-    store_slopes.wait()
 
 
 def local(fields, phases, residual, led_index):
     consts = [jnp.asarray(t) for t in tables()]
     scratch = [
+        pltpu.SMEM(led_index.shape, jnp.int32),
         pltpu.VMEM(fields.shape, F32),
         pltpu.VMEM(phases.shape, F32),
-        pltpu.VMEM(residual.shape, F32),
     ]
     slots = 2 * SLICES * LEDS
     scratch += [pltpu.VMEM(t.shape, t.dtype) for t in consts]
@@ -410,29 +400,30 @@
     scratch += [
         pltpu.VMEM((SLICES, GROUPS, ROWS, LANES), F32),
         pltpu.VMEM((SLICES, GROUPS, ROWS, LANES), F32),
-        pltpu.VMEM((SLICES, ROWS, LANES), F32),
-        pltpu.SemaphoreType.DMA((8,)),
+        pltpu.SemaphoreType.DMA((9,)),
         pltpu.SemaphoreType.DMA((slots,)),
         pltpu.SemaphoreType.DMA((slots,)),
         pltpu.SemaphoreType.DMA((SLICES,)),
         pltpu.SemaphoreType.DMA((SLICES,)),
-        pltpu.SemaphoreType.DMA((LEDS + 1,)),
+    ]
+    held = [
+        pltpu.with_memory_space_constraint(x, pltpu.HBM) for x in [led_index, fields, phases, residual] + consts
     ]
     anywhere = pl.BlockSpec(memory_space=pl.ANY)
     return pl.pallas_call(
         kernel,
         out_shape=(
-            jax.ShapeDtypeStruct((SLICES, ROWS, LANES), F32),
-            jax.ShapeDtypeStruct(residual.shape, F32),
+            pltpu.VMEM((SLICES, ROWS, LANES), F32),
+            pltpu.VMEM(residual.shape, F32),
         ),
-        in_specs=[pl.BlockSpec(memory_space=pltpu.SMEM)] + [anywhere] * 8,
-        out_specs=(anywhere, anywhere),
+        in_specs=[anywhere] * 9,
+        out_specs=(pl.BlockSpec(memory_space=pltpu.VMEM),) * 2,
         scratch_shapes=scratch,
         compiler_params=pltpu.CompilerParams(
             collective_id=0, has_side_effects=True, vmem_limit_bytes=VMEM_LIMIT
         ),
         name="adjoint",
-    )(led_index, fields, phases, residual, *consts)
+    )(*held)
 
 
 def solution(mesh):

time: 62.1 us -> 58.1 us (0.936)
  Pallas kernels: 58.3 us -> 56 us
  local copies, waits for them, and re-layouts: 2.99 us -> 1.31 us
    pallas_call x1, Pallas kernels: 58.3 us -> 56 us  [local(): pl.pallas_call(kernel, out_shape=(pltpu.VMEM((SLICES, ROWS, LANES), F32),...]
    unnamed x2, local copies, waits for them, and re-layouts: 2.99 us -> 1.31 us
where the time goes in v1:
time: 58.1 us; the launch traced here: 58 us
  Pallas kernels  56 us (96%)
  local copies, waits for them, and re-layouts  1.31 us (2%)
  between operations  0.64 us (1%)
    pallas_call x1, Pallas kernels, local(): pl.pallas_call(kernel, out_shape=(pltpu.VMEM((SLICES, ROWS, LANES), F32),...  56 us
    unnamed x2, local copies, waits for them, and re-layouts  1.31 us

profile of v1, /device:TPU:1, one launch (start us, length us, event | category | flops | bytes accessed | tf_op | source)
XLA Modules:
  0.0 58.0 jit_solution(15505540962623684573)
XLA Ops:
  0.6 56.0 %adjoint.1 = (f32[2,16,128]{2,1,0:T(8,128)S(1)}, f32[2,2,16,1024]{3,2,1,0:T(8,128)S(1)}) custom-call(s32[2]{0:T(128)} %led_hbm.1, f32[2,2,2,16,1024]{4,3,2,1,0:T(8,128)} %fields_hbm.1, f32[2,16,1024]{2,1,0:T(8,128)} %phases_hbm.1, f32[2,2,16,1024]{3,2,1,0:T(8,128)} %residual_hbm.1, f32[256,256]{1,0:T(8,128)} %constant.10.clone.wide_hbm, ...), custom_call_target="tpu_custom_call" | custom-call | tf_op jit(solution)/shard_map/adjoint/pallas_call | solution.py:413
  56.6 0.6 %copy.13 = f32[2,16,128]{2,1,0:T(8,128)} copy(f32[2,16,128]{2,1,0:T(8,128)S(1)} %get-tuple-element.2) | data formatting | bytes 32768
  57.2 0.7 %copy.14 = f32[2,2,16,1024]{3,2,1,0:T(8,128)} copy(f32[2,2,16,1024]{3,2,1,0:T(8,128)S(1)} %get-tuple-element.3) | data formatting | bytes 524288

commit v2 on v1

--- a/solution.py
+++ b/solution.py
@@ -17,6 +17,7 @@
 VMEM_LIMIT = 40 * 1024 * 1024
 ROWS = 16
 PEERS = 64
+OWNERS = 32
 GROUPS = 8
 LEDS = 2
 SLICES = 2
@@ -144,7 +145,7 @@
     stacked = jnp.concatenate([jnp.concatenate(blocks[c], axis=1) for c in range(2)], axis=0)
     mixed = dot3(long, split(stacked), ((1,), (0,)))
     rows = []
-    for k in range(2):
+    for k in range(4):
         re = mixed[:PEERS, LANES * k : LANES * (k + 1)]
         im = mixed[PEERS:, LANES * k : LANES * (k + 1)]
         rows.append(jnp.concatenate(twist(re, im, turn_cos, turn_sin), axis=1))
@@ -154,7 +155,7 @@
 def column_inverse(real, imag, turn_cos, turn_sin, long, short):
     mixed = dot3(split(jnp.concatenate([real, imag], axis=1)), short, ((1,), (0,)))
     first, second = [], []
-    for k in range(2):
+    for k in range(4):
         block = mixed[PEERS * k : PEERS * (k + 1)]
         re, im = twist(block[:, :LANES], block[:, LANES:], turn_cos, turn_sin)
         first.append(re)
@@ -168,7 +169,7 @@
 def filter_block(owner, k2lo, led):
     lane = lax.broadcasted_iota(jnp.int32, (PEERS, LANES), 1)
     v1 = lax.broadcasted_iota(jnp.int32, (PEERS, LANES), 0)
-    u = (lane >> 4) + 8 * (PEERS * k2lo + owner)
+    u = (lane >> 4) + 8 * (OWNERS * k2lo + owner)
     v = v1 + PEERS * (lane & (ROWS - 1))
     kx = (led // GRID - GRID // 2) * SHIFT
     ky = (led % GRID - GRID // 2) * SHIFT
@@ -183,12 +184,15 @@
     led_hbm, fields_hbm, phases_hbm, residual_hbm, wide_hbm, long_hbm, short_hbm, trow_hbm, tcol_hbm,
     slopes, wave,
     led_ref, fields, phases, wide_f32, long_f32, short_f32, trow, tcol, wide_ref, long_ref, short_ref,
-    filt, trans, out_box, in_box, slope_out, slope_in,
-    load_sem, send_sem, recv_sem, lsend_sem, lrecv_sem,
+    filt, trans, col_out, col_in, row_out, row_in, slope_out, slope_in,
+    load_sem, col_send_sem, col_recv_sem, row_send_sem, row_recv_sem, lsend_sem, lrecv_sem,
 ):
     me = lax.axis_index("row")
     group = lax.axis_index("led")
     my_y, my_w = me // 8, me % 8
+    my_x, my_z = my_w // 2, my_w % 2
+    my_led = lax.rem(my_x + my_y, 2)
+    my_owner = my_y * 4 + my_x // 2 * 2 + my_z
     led_peers = [lax.rem(group + d, GROUPS) for d in (4, 3, 5, 2, 6, 7, 1)]
 
     loads = [
@@ -229,63 +233,85 @@
     def halves(table):
         return table[0], table[1]
 
-    bases = [lax.rem(my_y + dy, 8) * 8 for dy in range(8)]
-
-    def send_tile(slot, peer):
+    near_far = (4, 3, 5, 2, 6, 1, 7, 0)
+
+    def copy_tile(source, target, send_sem, recv_sem, peer):
         pltpu.make_async_remote_copy(
-            src_ref=out_box.at[slot, peer],
-            dst_ref=in_box.at[slot, me],
-            send_sem=send_sem.at[slot],
-            recv_sem=recv_sem.at[slot],
+            src_ref=source,
+            dst_ref=target,
+            send_sem=send_sem,
+            recv_sem=recv_sem,
             device_id=(group, peer),
             device_id_type=MESH,
         ).start()
 
-    columns = [lax.rem(my_w + dw, 8) for dw in range(8)]
-
-    def send(slot):
+    def send_columns(turn, led):
+        target = col_in.at[turn, me]
+        sem = col_recv_sem.at[turn]
+
+        def to(dy, dx, dz):
+            y, half, z = lax.rem(my_y + dy, 8), lax.rem(my_x // 2 + dx, 2), lax.rem(my_z + dz, 2)
+            source = col_out.at[turn, led, y * 4 + half * 2 + z]
+            return source, y * 8 + half * 4 + lax.rem(led + y, 2) * 2 + z
+
+        for dx, dz in ((1, 1), (1, 0), (0, 1), (0, 0)):
+            for dy in near_far:
+                if dy + dx + dz > 0:
+                    source, peer = to(dy, dx, dz)
+                    copy_tile(source, target, col_send_sem.at[turn], sem, peer)
+        source, peer = to(0, 0, 0)
+
+        @pl.when(led == my_led)
+        def _():
+            pltpu.make_async_copy(source, target, sem).start()
+
+        @pl.when(led != my_led)
+        def _():
+            copy_tile(source, target, col_send_sem.at[turn], sem, peer)
+
+    def send_rows(turn):
+        target = row_in.at[turn, my_led, my_owner]
+        sem = row_recv_sem.at[turn, my_led]
         for dw in (5, 4, 3, 1, 7, 2, 6, 0):
-            for dy in (4, 3, 5, 2, 6, 1, 7, 0):
+            for dy in near_far:
                 if dw + dy > 0:
-                    send_tile(slot, bases[dy] + columns[dw])
-        pltpu.make_async_copy(out_box.at[slot, me], in_box.at[slot, me], recv_sem.at[slot]).start()
-
-    def put(values, slot):
-        flat = out_box.at[slot].reshape(PEERS * 4, LANES)
-        for j in range(4):
-            flat[pl.ds(j, PEERS, stride=4), :] = values[j]
-
-    def arrived(slot):
-        whole = in_box.at[slot]
-        pltpu.make_async_copy(whole, whole, recv_sem.at[slot]).wait()
-        flat = whole.reshape(PEERS * 4, LANES)
-        return [flat[pl.ds(j, PEERS, stride=4), :] for j in range(4)]
+                    peer = lax.rem(my_y + dy, 8) * 8 + lax.rem(my_w + dw, 8)
+                    copy_tile(row_out.at[turn, peer], target, row_send_sem.at[turn], sem, peer)
+        pltpu.make_async_copy(row_out.at[turn, me], target, sem).start()
+
+    def put(values, box, peers):
+        flat = box.reshape(peers * TILE, LANES)
+        for j in range(TILE):
+            flat[pl.ds(j, peers, stride=TILE), :] = values[j]
+
+    def arrived(box, sem, peers):
+        pltpu.make_async_copy(box, box, sem).wait()
+        flat = box.reshape(peers * TILE, LANES)
+        return [flat[pl.ds(j, peers, stride=TILE), :] for j in range(TILE)]
 
     def columns_of(ref, c):
         return [ref[c, :, LANES * a : LANES * (a + 1)] for a in range(8)]
 
-    def to_columns(led, slot):
+    def to_columns(turn, led):
         seed = wave.at[led]
         spectrum = row_forward(
             columns_of(seed, 0), columns_of(seed, 1), turn_cos, turn_sin, halves(wide_ref)
         )
-        put([spectrum[PEERS * j : PEERS * (j + 1)] for j in range(4)], slot)
-
-    def slot_of(turn, way, led):
-        return (2 * turn + way) * LEDS + led
-
-    def column_pass(turn, led):
-        tiles = arrived(slot_of(turn, 0, led))
-        spectrum = column_forward([tiles[:2], tiles[2:]], tcol[0], tcol[1], halves(long_ref), halves(short_ref))
-        real, imag = twist(spectrum[:, :LANES], spectrum[:, LANES:], filt[led, 0], filt[led, 1])
+        values = [spectrum[OWNERS * j : OWNERS * (j + 1)] for j in range(TILE)]
+        put(values, col_out.at[turn, led], OWNERS)
+
+    def column_pass(turn):
+        tiles = arrived(col_in.at[turn], col_recv_sem.at[turn], PEERS)
+        spectrum = column_forward([tiles[:4], tiles[4:]], tcol[0], tcol[1], halves(long_ref), halves(short_ref))
+        real, imag = twist(spectrum[:, :LANES], spectrum[:, LANES:], filt[0], filt[1])
         back = column_inverse(imag, real, tcol[0], tcol[1], halves(long_ref), halves(short_ref))
         values = [
             back[PEERS * (1 - c) : PEERS * (2 - c), LANES * k : LANES * (k + 1)]
             for c in range(2)
-            for k in range(2)
+            for k in range(4)
         ]
-        put(values, slot_of(turn, 1, led))
-        send(slot_of(turn, 1, led))
+        put(values, row_out.at[turn], PEERS)
+        send_rows(turn)
 
     def send_slopes(turn):
         for peer in led_peers:
@@ -303,8 +329,8 @@
 
     def from_columns(turn, led):
         layer = SLICES - 1 - turn
-        tiles = arrived(slot_of(turn, 1, led))
-        swapped = jnp.concatenate([tiles[2], tiles[3], tiles[0], tiles[1]], axis=0)
+        tiles = arrived(row_in.at[turn, led], row_recv_sem.at[turn, led], OWNERS)
+        swapped = jnp.concatenate(tiles[4:] + tiles[:4], axis=0)
         imag, real = row_inverse(swapped, turn_cos, turn_sin, halves(wide_ref))
         for a in range(8):
             cols = slice(LANES * a, LANES * (a + 1))
@@ -333,13 +359,13 @@
 
             @pl.when(phase < SLICES)
             def _():
-                to_columns(led, slot_of(phase, 0, led))
+                to_columns(phase, led)
 
                 @pl.when(phase + led == 0)
                 def _():
                     pl.semaphore_wait(barrier, PEERS - 1 + GROUPS - 1)
 
-                send(slot_of(phase, 0, led))
+                send_columns(phase, led)
 
             @pl.when(phase > 0)
             def _():
@@ -353,11 +379,10 @@
         def _():
             for load in loads[3:]:
                 load.wait()
-            for led in range(LEDS):
-                for k in range(2):
-                    cosine, sine = filter_block(me, k, led_ref[led])
-                    filt[led, 0, PEERS * k : PEERS * (k + 1), :] = cosine
-                    filt[led, 1, PEERS * k : PEERS * (k + 1), :] = sine
+            for k in range(4):
+                cosine, sine = filter_block(my_owner, k, led_ref[my_led])
+                filt[0, PEERS * k : PEERS * (k + 1), :] = cosine
+                filt[1, PEERS * k : PEERS * (k + 1), :] = sine
             long_ref[0], long_ref[1] = split(long_f32[...])
             short_ref[0], short_ref[1] = split(short_f32[...])
             for layer in range(SLICES):
@@ -367,16 +392,15 @@
 
         @pl.when(phase < SLICES)
         def _():
-            @pl.loop(0, LEDS)
-            def _(led):
-                column_pass(phase, led)
+            column_pass(phase)
 
     for turn in range(SLICES):
         pltpu.make_async_copy(slope_in.at[turn], slope_in.at[turn], lrecv_sem.at[turn]).wait()
         slopes[SLICES - 1 - turn] = jnp.sum(slope_in[turn], axis=0) * (1.0 / (LEDS * GROUPS))
-    for slot in range(2 * SLICES * LEDS):
-        sent = out_box.at[slot, pl.ds(0, PEERS - 1)]
-        pltpu.make_async_copy(sent, sent, send_sem.at[slot]).wait()
+    for turn in range(SLICES):
+        sent = row_out.at[turn, pl.ds(0, PEERS - 1)]
+        for sem in (row_send_sem, col_send_sem):
+            pltpu.make_async_copy(sent, sent, sem.at[turn]).wait()
     for turn in range(SLICES):
         sent = slope_out.at[turn, pl.ds(0, GROUPS - 1)]
         pltpu.make_async_copy(sent, sent, lsend_sem.at[turn]).wait()
@@ -389,20 +413,23 @@
         pltpu.VMEM(fields.shape, F32),
         pltpu.VMEM(phases.shape, F32),
     ]
-    slots = 2 * SLICES * LEDS
     scratch += [pltpu.VMEM(t.shape, t.dtype) for t in consts]
     scratch += [pltpu.VMEM((2,) + t.shape, BF16) for t in consts[:3]]
     scratch += [
-        pltpu.VMEM((LEDS, 2, LANES, LANES), F32),
+        pltpu.VMEM((2, 4 * PEERS, LANES), F32),
         pltpu.VMEM((SLICES, 2, ROWS, N), F32),
     ]
-    scratch += [pltpu.VMEM((slots, PEERS, 4, LANES), F32)] * 2
+    to_col = pltpu.VMEM((SLICES, LEDS, OWNERS, TILE, LANES), F32)
+    to_row = pltpu.VMEM((SLICES, PEERS, TILE, LANES), F32)
+    scratch += [to_col, to_row, to_row, to_col]
     scratch += [
         pltpu.VMEM((SLICES, GROUPS, ROWS, LANES), F32),
         pltpu.VMEM((SLICES, GROUPS, ROWS, LANES), F32),
         pltpu.SemaphoreType.DMA((9,)),
-        pltpu.SemaphoreType.DMA((slots,)),
-        pltpu.SemaphoreType.DMA((slots,)),
+        pltpu.SemaphoreType.DMA((SLICES,)),
+        pltpu.SemaphoreType.DMA((SLICES,)),
+        pltpu.SemaphoreType.DMA((SLICES,)),
+        pltpu.SemaphoreType.DMA((SLICES, LEDS)),
         pltpu.SemaphoreType.DMA((SLICES,)),
         pltpu.SemaphoreType.DMA((SLICES,)),
     ]

time: 58.1 us -> 59 us (1.015)
  Pallas kernels: 56 us -> 56.9 us
    pallas_call x1, Pallas kernels: 56 us -> 56.9 us  [local(): pl.pallas_call(kernel, out_shape=(pltpu.VMEM((SLICES, ROWS, LANES), F32),...]
where the time goes in v2:
time: 59 us; the launch traced here: 58.8 us
  Pallas kernels  56.9 us (96%)
  local copies, waits for them, and re-layouts  1.31 us (2%)
  between operations  0.64 us (1%)
    pallas_call x1, Pallas kernels, local(): pl.pallas_call(kernel, out_shape=(pltpu.VMEM((SLICES, ROWS, LANES), F32),...  56.9 us
    unnamed x2, local copies, waits for them, and re-layouts  1.31 us

profile of v2, /device:TPU:1, one launch (start us, length us, event | category | flops | bytes accessed | tf_op | source)
XLA Modules:
  0.0 58.8 jit_solution(17698730478023666592)
XLA Ops:
  0.6 56.9 %adjoint.1 = (f32[2,16,128]{2,1,0:T(8,128)S(1)}, f32[2,2,16,1024]{3,2,1,0:T(8,128)S(1)}) custom-call(s32[2]{0:T(128)} %led_hbm.1, f32[2,2,2,16,1024]{4,3,2,1,0:T(8,128)} %fields_hbm.1, f32[2,16,1024]{2,1,0:T(8,128)} %phases_hbm.1, f32[2,2,16,1024]{3,2,1,0:T(8,128)} %residual_hbm.1, f32[256,256]{1,0:T(8,128)} %constant.10.clone.wide_hbm, ...), custom_call_target="tpu_custom_call" | custom-call | tf_op jit(solution)/shard_map/adjoint/pallas_call | solution.py:440
  57.5 0.6 %copy.13 = f32[2,16,128]{2,1,0:T(8,128)} copy(f32[2,16,128]{2,1,0:T(8,128)S(1)} %get-tuple-element.2) | data formatting | bytes 32768
  58.1 0.7 %copy.14 = f32[2,2,16,1024]{3,2,1,0:T(8,128)} copy(f32[2,2,16,1024]{3,2,1,0:T(8,128)S(1)} %get-tuple-element.3) | data formatting | bytes 524288

commit v3 on v2

--- a/solution.py
+++ b/solution.py
@@ -13,11 +13,12 @@
 DZ = 64
 SHIFT = 10
 LANES = 128
-TILE = 8
 VMEM_LIMIT = 40 * 1024 * 1024
 ROWS = 16
 PEERS = 64
 OWNERS = 32
+HALVES = 2
+PART = 4
 GROUPS = 8
 LEDS = 2
 SLICES = 2
@@ -44,7 +45,7 @@
     eye = np.eye(LANES // ROWS)
     cos, sin = np.kron(eye, cos), np.kron(eye, sin)
     short = np.block([[cos, -sin], [sin, cos]]).astype(np.float32)
-    angle = 2.0 * np.pi * np.outer(np.arange(TILE), np.arange(LANES)) / N
+    angle = 2.0 * np.pi * np.outer(np.arange(8), np.arange(LANES)) / N
     turn_rows = np.concatenate([np.cos(angle), np.sin(angle)]).astype(np.float32)
     angle = 2.0 * np.pi * np.outer(np.arange(PEERS), np.arange(LANES) % ROWS) / N
     turn_cols = np.stack([np.cos(angle), np.sin(angle)]).astype(np.float32)
@@ -145,7 +146,7 @@
     stacked = jnp.concatenate([jnp.concatenate(blocks[c], axis=1) for c in range(2)], axis=0)
     mixed = dot3(long, split(stacked), ((1,), (0,)))
     rows = []
-    for k in range(4):
+    for k in range(2):
         re = mixed[:PEERS, LANES * k : LANES * (k + 1)]
         im = mixed[PEERS:, LANES * k : LANES * (k + 1)]
         rows.append(jnp.concatenate(twist(re, im, turn_cos, turn_sin), axis=1))
@@ -155,7 +156,7 @@
 def column_inverse(real, imag, turn_cos, turn_sin, long, short):
     mixed = dot3(split(jnp.concatenate([real, imag], axis=1)), short, ((1,), (0,)))
     first, second = [], []
-    for k in range(4):
+    for k in range(2):
         block = mixed[PEERS * k : PEERS * (k + 1)]
         re, im = twist(block[:, :LANES], block[:, LANES:], turn_cos, turn_sin)
         first.append(re)
@@ -233,7 +234,17 @@
     def halves(table):
         return table[0], table[1]
 
-    near_far = (4, 3, 5, 2, 6, 1, 7, 0)
+    def away(step, ring):
+        return min(step, ring - step)
+
+    owner_steps = sorted(
+        [(dy, dx, dz) for dy in (4, 3, 5, 2, 6, 1, 7, 0) for dx in (1, 0) for dz in (1, 0)],
+        key=lambda step: -(away(step[0], 8) + 1.5 * step[1] + step[2]),
+    )[:-1]
+    row_steps = sorted(
+        [(dy, dx, dz) for dy in (4, 3, 5, 2, 6, 1, 7, 0) for dx in (2, 1, 3, 0) for dz in (1, 0)],
+        key=lambda step: -(away(step[0], 8) + away(step[1], 4) + step[2]),
+    )[:-1]
 
     def copy_tile(source, target, send_sem, recv_sem, peer):
         pltpu.make_async_remote_copy(
@@ -245,20 +256,19 @@
             device_id_type=MESH,
         ).start()
 
-    def send_columns(turn, led):
-        target = col_in.at[turn, me]
-        sem = col_recv_sem.at[turn]
+    def send_columns(turn, led, half):
+        target = col_in.at[turn, half, me]
+        sem = col_recv_sem.at[turn, half]
+        sent = col_send_sem.at[turn, half]
 
         def to(dy, dx, dz):
-            y, half, z = lax.rem(my_y + dy, 8), lax.rem(my_x // 2 + dx, 2), lax.rem(my_z + dz, 2)
-            source = col_out.at[turn, led, y * 4 + half * 2 + z]
-            return source, y * 8 + half * 4 + lax.rem(led + y, 2) * 2 + z
-
-        for dx, dz in ((1, 1), (1, 0), (0, 1), (0, 0)):
-            for dy in near_far:
-                if dy + dx + dz > 0:
-                    source, peer = to(dy, dx, dz)
-                    copy_tile(source, target, col_send_sem.at[turn], sem, peer)
+            y, pair, z = lax.rem(my_y + dy, 8), lax.rem(my_x // 2 + dx, 2), lax.rem(my_z + dz, 2)
+            source = col_out.at[turn, half, led, y * 4 + pair * 2 + z]
+            return source, y * 8 + pair * 4 + lax.rem(led + y, 2) * 2 + z
+
+        for step in owner_steps:
+            source, peer = to(*step)
+            copy_tile(source, target, sent, sem, peer)
         source, peer = to(0, 0, 0)
 
         @pl.when(led == my_led)
@@ -267,27 +277,26 @@
 
         @pl.when(led != my_led)
         def _():
-            copy_tile(source, target, col_send_sem.at[turn], sem, peer)
-
-    def send_rows(turn):
-        target = row_in.at[turn, my_led, my_owner]
-        sem = row_recv_sem.at[turn, my_led]
-        for dw in (5, 4, 3, 1, 7, 2, 6, 0):
-            for dy in near_far:
-                if dw + dy > 0:
-                    peer = lax.rem(my_y + dy, 8) * 8 + lax.rem(my_w + dw, 8)
-                    copy_tile(row_out.at[turn, peer], target, row_send_sem.at[turn], sem, peer)
-        pltpu.make_async_copy(row_out.at[turn, me], target, sem).start()
+            copy_tile(source, target, sent, sem, peer)
+
+    def send_rows(turn, half):
+        target = row_in.at[turn, half, my_led, my_owner]
+        sem = row_recv_sem.at[turn, half, my_led]
+        for dy, dx, dz in row_steps:
+            y, x, z = lax.rem(my_y + dy, 8), lax.rem(my_x + dx, 4), lax.rem(my_z + dz, 2)
+            peer = y * 8 + x * 2 + z
+            copy_tile(row_out.at[turn, half, peer], target, row_send_sem.at[turn, half], sem, peer)
+        pltpu.make_async_copy(row_out.at[turn, half, me], target, sem).start()
 
     def put(values, box, peers):
-        flat = box.reshape(peers * TILE, LANES)
-        for j in range(TILE):
-            flat[pl.ds(j, peers, stride=TILE), :] = values[j]
+        flat = box.reshape(peers * PART, LANES)
+        for j in range(PART):
+            flat[pl.ds(j, peers, stride=PART), :] = values[j]
 
     def arrived(box, sem, peers):
         pltpu.make_async_copy(box, box, sem).wait()
-        flat = box.reshape(peers * TILE, LANES)
-        return [flat[pl.ds(j, peers, stride=TILE), :] for j in range(TILE)]
+        flat = box.reshape(peers * PART, LANES)
+        return [flat[pl.ds(j, peers, stride=PART), :] for j in range(PART)]
 
     def columns_of(ref, c):
         return [ref[c, :, LANES * a : LANES * (a + 1)] for a in range(8)]
@@ -297,21 +306,22 @@
         spectrum = row_forward(
             columns_of(seed, 0), columns_of(seed, 1), turn_cos, turn_sin, halves(wide_ref)
         )
-        values = [spectrum[OWNERS * j : OWNERS * (j + 1)] for j in range(TILE)]
-        put(values, col_out.at[turn, led], OWNERS)
-
-    def column_pass(turn):
-        tiles = arrived(col_in.at[turn], col_recv_sem.at[turn], PEERS)
-        spectrum = column_forward([tiles[:4], tiles[4:]], tcol[0], tcol[1], halves(long_ref), halves(short_ref))
-        real, imag = twist(spectrum[:, :LANES], spectrum[:, LANES:], filt[0], filt[1])
+        values = [spectrum[OWNERS * j : OWNERS * (j + 1)] for j in range(2 * PART)]
+        put(values[0:2] + values[4:6], col_out.at[turn, 0, led], OWNERS)
+        put(values[2:4] + values[6:8], col_out.at[turn, 1, led], OWNERS)
+
+    def column_pass(turn, half):
+        tiles = arrived(col_in.at[turn, half], col_recv_sem.at[turn, half], PEERS)
+        spectrum = column_forward([tiles[:2], tiles[2:]], tcol[0], tcol[1], halves(long_ref), halves(short_ref))
+        real, imag = twist(spectrum[:, :LANES], spectrum[:, LANES:], filt[half, 0], filt[half, 1])
         back = column_inverse(imag, real, tcol[0], tcol[1], halves(long_ref), halves(short_ref))
         values = [
             back[PEERS * (1 - c) : PEERS * (2 - c), LANES * k : LANES * (k + 1)]
             for c in range(2)
-            for k in range(4)
+            for k in range(2)
         ]
-        put(values, row_out.at[turn], PEERS)
-        send_rows(turn)
+        put(values, row_out.at[turn, half], PEERS)
+        send_rows(turn, half)
 
     def send_slopes(turn):
         for peer in led_peers:
@@ -329,8 +339,11 @@
 
     def from_columns(turn, led):
         layer = SLICES - 1 - turn
-        tiles = arrived(row_in.at[turn, led], row_recv_sem.at[turn, led], OWNERS)
-        swapped = jnp.concatenate(tiles[4:] + tiles[:4], axis=0)
+        first, second = [
+            arrived(row_in.at[turn, half, led], row_recv_sem.at[turn, half, led], OWNERS)
+            for half in range(HALVES)
+        ]
+        swapped = jnp.concatenate(first[2:] + second[2:] + first[:2] + second[:2], axis=0)
         imag, real = row_inverse(swapped, turn_cos, turn_sin, halves(wide_ref))
         for a in range(8):
             cols = slice(LANES * a, LANES * (a + 1))
@@ -365,7 +378,8 @@
                 def _():
                     pl.semaphore_wait(barrier, PEERS - 1 + GROUPS - 1)
 
-                send_columns(phase, led)
+                for half in range(HALVES):
+                    send_columns(phase, led, half)
 
             @pl.when(phase > 0)
             def _():
@@ -381,8 +395,8 @@
                 load.wait()
             for k in range(4):
                 cosine, sine = filter_block(my_owner, k, led_ref[my_led])
-                filt[0, PEERS * k : PEERS * (k + 1), :] = cosine
-                filt[1, PEERS * k : PEERS * (k + 1), :] = sine
+                filt[k // 2, 0, PEERS * (k % 2) : PEERS * (k % 2 + 1), :] = cosine
+                filt[k // 2, 1, PEERS * (k % 2) : PEERS * (k % 2 + 1), :] = sine
             long_ref[0], long_ref[1] = split(long_f32[...])
             short_ref[0], short_ref[1] = split(short_f32[...])
             for layer in range(SLICES):
@@ -392,15 +406,18 @@
 
         @pl.when(phase < SLICES)
         def _():
-            column_pass(phase)
+            @pl.loop(0, HALVES)
+            def _(half):
+                column_pass(phase, half)
 
     for turn in range(SLICES):
         pltpu.make_async_copy(slope_in.at[turn], slope_in.at[turn], lrecv_sem.at[turn]).wait()
         slopes[SLICES - 1 - turn] = jnp.sum(slope_in[turn], axis=0) * (1.0 / (LEDS * GROUPS))
     for turn in range(SLICES):
-        sent = row_out.at[turn, pl.ds(0, PEERS - 1)]
-        for sem in (row_send_sem, col_send_sem):
-            pltpu.make_async_copy(sent, sent, sem.at[turn]).wait()
+        for half in range(HALVES):
+            sent = row_out.at[turn, half, pl.ds(0, PEERS - 1)]
+            for sem in (row_send_sem, col_send_sem):
+                pltpu.make_async_copy(sent, sent, sem.at[turn, half]).wait()
     for turn in range(SLICES):
         sent = slope_out.at[turn, pl.ds(0, GROUPS - 1)]
         pltpu.make_async_copy(sent, sent, lsend_sem.at[turn]).wait()
@@ -416,20 +433,20 @@
     scratch += [pltpu.VMEM(t.shape, t.dtype) for t in consts]
     scratch += [pltpu.VMEM((2,) + t.shape, BF16) for t in consts[:3]]
     scratch += [
-        pltpu.VMEM((2, 4 * PEERS, LANES), F32),
+        pltpu.VMEM((HALVES, 2, 2 * PEERS, LANES), F32),
         pltpu.VMEM((SLICES, 2, ROWS, N), F32),
     ]
-    to_col = pltpu.VMEM((SLICES, LEDS, OWNERS, TILE, LANES), F32)
-    to_row = pltpu.VMEM((SLICES, PEERS, TILE, LANES), F32)
+    to_col = pltpu.VMEM((SLICES, HALVES, LEDS, OWNERS, PART, LANES), F32)
+    to_row = pltpu.VMEM((SLICES, HALVES, PEERS, PART, LANES), F32)
     scratch += [to_col, to_row, to_row, to_col]
     scratch += [
         pltpu.VMEM((SLICES, GROUPS, ROWS, LANES), F32),
         pltpu.VMEM((SLICES, GROUPS, ROWS, LANES), F32),
         pltpu.SemaphoreType.DMA((9,)),
-        pltpu.SemaphoreType.DMA((SLICES,)),
-        pltpu.SemaphoreType.DMA((SLICES,)),
-        pltpu.SemaphoreType.DMA((SLICES,)),
-        pltpu.SemaphoreType.DMA((SLICES, LEDS)),
+        pltpu.SemaphoreType.DMA((SLICES, HALVES)),
+        pltpu.SemaphoreType.DMA((SLICES, HALVES)),
+        pltpu.SemaphoreType.DMA((SLICES, HALVES)),
+        pltpu.SemaphoreType.DMA((SLICES, HALVES, LEDS)),
         pltpu.SemaphoreType.DMA((SLICES,)),
         pltpu.SemaphoreType.DMA((SLICES,)),
     ]

time: 59 us -> 57.4 us (0.973)
  Pallas kernels: 56.9 us -> 55.3 us
    pallas_call x1, Pallas kernels: 56.9 us -> 55.3 us  [local(): pl.pallas_call(kernel, out_shape=(pltpu.VMEM((SLICES, ROWS, LANES), F32),...]
where the time goes in v3:
time: 57.4 us; the launch traced here: 57.3 us
  Pallas kernels  55.3 us (96%)
  local copies, waits for them, and re-layouts  1.31 us (2%)
  between operations  0.64 us (1%)
    pallas_call x1, Pallas kernels, local(): pl.pallas_call(kernel, out_shape=(pltpu.VMEM((SLICES, ROWS, LANES), F32),...  55.3 us
    unnamed x2, local copies, waits for them, and re-layouts  1.31 us

profile of v3, /device:TPU:1, one launch (start us, length us, event | category | flops | bytes accessed | tf_op | source)
XLA Modules:
  0.0 57.3 jit_solution(17515848040087946851)
XLA Ops:
  0.6 55.3 %adjoint.1 = (f32[2,16,128]{2,1,0:T(8,128)S(1)}, f32[2,2,16,1024]{3,2,1,0:T(8,128)S(1)}) custom-call(s32[2]{0:T(128)} %led_hbm.1, f32[2,2,2,16,1024]{4,3,2,1,0:T(8,128)} %fields_hbm.1, f32[2,16,1024]{2,1,0:T(8,128)} %phases_hbm.1, f32[2,2,16,1024]{3,2,1,0:T(8,128)} %residual_hbm.1, f32[256,256]{1,0:T(8,128)} %constant.10.clone.wide_hbm, ...), custom_call_target="tpu_custom_call" | custom-call | tf_op jit(solution)/shard_map/adjoint/pallas_call | solution.py:457
  55.9 0.6 %copy.13 = f32[2,16,128]{2,1,0:T(8,128)} copy(f32[2,16,128]{2,1,0:T(8,128)S(1)} %get-tuple-element.2) | data formatting | bytes 32768
  56.6 0.7 %copy.14 = f32[2,2,16,1024]{3,2,1,0:T(8,128)} copy(f32[2,2,16,1024]{3,2,1,0:T(8,128)S(1)} %get-tuple-element.3) | data formatting | bytes 524288

commit v4 on v3

--- a/solution.py
+++ b/solution.py
@@ -186,7 +186,7 @@
     slopes, wave,
     led_ref, fields, phases, wide_f32, long_f32, short_f32, trow, tcol, wide_ref, long_ref, short_ref,
     filt, trans, col_out, col_in, row_out, row_in, slope_out, slope_in,
-    load_sem, col_send_sem, col_recv_sem, row_send_sem, row_recv_sem, lsend_sem, lrecv_sem,
+    ready_sem, load_sem, col_send_sem, col_recv_sem, row_send_sem, row_recv_sem, lsend_sem, lrecv_sem,
 ):
     me = lax.axis_index("row")
     group = lax.axis_index("led")
@@ -217,13 +217,15 @@
 
     barrier = pltpu.get_barrier_semaphore()
 
-    @pl.loop(1, PEERS)
-    def _(step):
-        peer = lax.rem(me + step, PEERS)
+    w_peers = [my_y * 8 + lax.rem(my_w + d, 8) for d in range(1, 8)]
+    y_peers = [lax.rem(my_y + d, 8) * 8 + my_w for d in range(1, 8)]
+    for peer in y_peers + w_peers:
         pl.semaphore_signal(barrier, inc=1, device_id=(group, peer), device_id_type=MESH)
-
     for peer in led_peers:
         pl.semaphore_signal(barrier, inc=1, device_id=(peer, me), device_id_type=MESH)
+    pl.semaphore_wait(barrier, 21)
+    for peer in w_peers:
+        pl.semaphore_signal(ready_sem, inc=1, device_id=(group, peer), device_id_type=MESH)
 
     for load in loads[:3]:
         load.wait()
@@ -376,7 +378,7 @@
 
                 @pl.when(phase + led == 0)
                 def _():
-                    pl.semaphore_wait(barrier, PEERS - 1 + GROUPS - 1)
+                    pl.semaphore_wait(ready_sem, 7)
 
                 for half in range(HALVES):
                     send_columns(phase, led, half)
@@ -421,6 +423,17 @@
     for turn in range(SLICES):
         sent = slope_out.at[turn, pl.ds(0, GROUPS - 1)]
         pltpu.make_async_copy(sent, sent, lsend_sem.at[turn]).wait()
+
+
+def emit_kernel(slopes_in, wave_in, slopes_ref, wave_ref, sem):
+    copies = [
+        pltpu.make_async_copy(wave_in, wave_ref, sem.at[0]),
+        pltpu.make_async_copy(slopes_in, slopes_ref, sem.at[1]),
+    ]
+    for copy in copies:
+        copy.start()
+    for copy in copies:
+        copy.wait()
 
 
 def local(fields, phases, residual, led_index):
@@ -442,6 +455,7 @@
     scratch += [
         pltpu.VMEM((SLICES, GROUPS, ROWS, LANES), F32),
         pltpu.VMEM((SLICES, GROUPS, ROWS, LANES), F32),
+        pltpu.SemaphoreType.REGULAR,
         pltpu.SemaphoreType.DMA((9,)),
         pltpu.SemaphoreType.DMA((SLICES, HALVES)),
         pltpu.SemaphoreType.DMA((SLICES, HALVES)),
@@ -454,7 +468,7 @@
         pltpu.with_memory_space_constraint(x, pltpu.HBM) for x in [led_index, fields, phases, residual] + consts
     ]
     anywhere = pl.BlockSpec(memory_space=pl.ANY)
-    return pl.pallas_call(
+    results = pl.pallas_call(
         kernel,
         out_shape=(
             pltpu.VMEM((SLICES, ROWS, LANES), F32),
@@ -468,6 +482,17 @@
         ),
         name="adjoint",
     )(*held)
+    return pl.pallas_call(
+        emit_kernel,
+        out_shape=(
+            pltpu.HBM((SLICES, ROWS, LANES), F32),
+            pltpu.HBM(residual.shape, F32),
+        ),
+        in_specs=[anywhere] * 2,
+        out_specs=(anywhere, anywhere),
+        scratch_shapes=[pltpu.SemaphoreType.DMA((2,))],
+        name="emit",
+    )(*[pltpu.with_memory_space_constraint(x, pltpu.VMEM) for x in results])
 
 
 def solution(mesh):

time: 57.4 us -> 57.2 us (level)
  local copies, waits for them, and re-layouts: 1.31 us -> 0 us
  Pallas kernels: 55.3 us -> 56.5 us
    unnamed x2 -> x0, local copies, waits for them, and re-layouts: 1.31 us -> none
    pallas_call x0 -> x1, Pallas kernels: none -> 0.72 us  [local(): pl.pallas_call(emit_kernel, out_shape=(pltpu.HBM((SLICES, ROWS, LANES), F...]
where the time goes in v4:
time: 57.2 us; the launch traced here: 57.1 us
  Pallas kernels  56.5 us (99%)
  between operations  0.64 us (1%)
    pallas_call x1, Pallas kernels, local(): pl.pallas_call(kernel, out_shape=(pltpu.VMEM((SLICES, ROWS, LANES), F32),...  55.8 us

profile of v4, /device:TPU:1, one launch (start us, length us, event | category | flops | bytes accessed | tf_op | source)
XLA Modules:
  0.0 57.1 jit_solution(4881021700094689492)
XLA Ops:
  0.6 55.8 %adjoint.1 = (f32[2,16,128]{2,1,0:T(8,128)S(1)}, f32[2,2,16,1024]{3,2,1,0:T(8,128)S(1)}) custom-call(s32[2]{0:T(128)} %led_hbm.1, f32[2,2,2,16,1024]{4,3,2,1,0:T(8,128)} %fields_hbm.1, f32[2,16,1024]{2,1,0:T(8,128)} %phases_hbm.1, f32[2,2,16,1024]{3,2,1,0:T(8,128)} %residual_hbm.1, f32[256,256]{1,0:T(8,128)} %constant.10.clone.wide_hbm, ...), custom_call_target="tpu_custom_call" | custom-call | tf_op jit(solution)/shard_map/adjoint/pallas_call | solution.py:471
  56.4 0.7 %emit.1 = (f32[2,16,128]{2,1,0:T(8,128)}, f32[2,2,16,1024]{3,2,1,0:T(8,128)}) custom-call(f32[2,16,128]{2,1,0:T(8,128)S(1)} %get-tuple-element.4.slopes_in, f32[2,2,16,1024]{3,2,1,0:T(8,128)S(1)} %get-tuple-element.5.wave_in), custom_call_target="tpu_custom_call" | custom-call | tf_op jit(solution)/shard_map/emit/pallas_call | solution.py:485

commit v5 on v4

--- a/solution.py
+++ b/solution.py
@@ -186,7 +186,7 @@
     slopes, wave,
     led_ref, fields, phases, wide_f32, long_f32, short_f32, trow, tcol, wide_ref, long_ref, short_ref,
     filt, trans, col_out, col_in, row_out, row_in, slope_out, slope_in,
-    ready_sem, load_sem, col_send_sem, col_recv_sem, row_send_sem, row_recv_sem, lsend_sem, lrecv_sem,
+    load_sem, col_send_sem, col_recv_sem, row_send_sem, row_recv_sem, lsend_sem, lrecv_sem,
 ):
     me = lax.axis_index("row")
     group = lax.axis_index("led")
@@ -217,15 +217,13 @@
 
     barrier = pltpu.get_barrier_semaphore()
 
-    w_peers = [my_y * 8 + lax.rem(my_w + d, 8) for d in range(1, 8)]
-    y_peers = [lax.rem(my_y + d, 8) * 8 + my_w for d in range(1, 8)]
-    for peer in y_peers + w_peers:
+    @pl.loop(1, PEERS)
+    def _(step):
+        peer = lax.rem(me + step, PEERS)
         pl.semaphore_signal(barrier, inc=1, device_id=(group, peer), device_id_type=MESH)
+
     for peer in led_peers:
         pl.semaphore_signal(barrier, inc=1, device_id=(peer, me), device_id_type=MESH)
-    pl.semaphore_wait(barrier, 21)
-    for peer in w_peers:
-        pl.semaphore_signal(ready_sem, inc=1, device_id=(group, peer), device_id_type=MESH)
 
     for load in loads[:3]:
         load.wait()
@@ -235,6 +233,10 @@
 
     def halves(table):
         return table[0], table[1]
+
+    way = 1 - 2 * lax.rem(group, 2)
+    ys = [lax.rem(my_y + 8 + way * dy, 8) for dy in range(8)]
+    xs = [lax.rem(my_x + 4 + way * dx, 4) for dx in range(4)]
 
     def away(step, ring):
         return min(step, ring - step)
@@ -264,7 +266,7 @@
         sent = col_send_sem.at[turn, half]
 
         def to(dy, dx, dz):
-            y, pair, z = lax.rem(my_y + dy, 8), lax.rem(my_x // 2 + dx, 2), lax.rem(my_z + dz, 2)
+            y, pair, z = ys[dy], lax.rem(my_x // 2 + dx, 2), lax.rem(my_z + dz, 2)
             source = col_out.at[turn, half, led, y * 4 + pair * 2 + z]
             return source, y * 8 + pair * 4 + lax.rem(led + y, 2) * 2 + z
 
@@ -285,7 +287,7 @@
         target = row_in.at[turn, half, my_led, my_owner]
         sem = row_recv_sem.at[turn, half, my_led]
         for dy, dx, dz in row_steps:
-            y, x, z = lax.rem(my_y + dy, 8), lax.rem(my_x + dx, 4), lax.rem(my_z + dz, 2)
+            y, x, z = ys[dy], xs[dx], lax.rem(my_z + dz, 2)
             peer = y * 8 + x * 2 + z
             copy_tile(row_out.at[turn, half, peer], target, row_send_sem.at[turn, half], sem, peer)
         pltpu.make_async_copy(row_out.at[turn, half, me], target, sem).start()
@@ -378,7 +380,7 @@
 
                 @pl.when(phase + led == 0)
                 def _():
-                    pl.semaphore_wait(ready_sem, 7)
+                    pl.semaphore_wait(barrier, PEERS - 1 + GROUPS - 1)
 
                 for half in range(HALVES):
                     send_columns(phase, led, half)
@@ -455,7 +457,6 @@
     scratch += [
         pltpu.VMEM((SLICES, GROUPS, ROWS, LANES), F32),
         pltpu.VMEM((SLICES, GROUPS, ROWS, LANES), F32),
-        pltpu.SemaphoreType.REGULAR,
         pltpu.SemaphoreType.DMA((9,)),
         pltpu.SemaphoreType.DMA((SLICES, HALVES)),
         pltpu.SemaphoreType.DMA((SLICES, HALVES)),

time: 57.2 us -> 56.8 us (level)
  no operation moved by 1% of the time
where the time goes in v5:
time: 56.8 us; the launch traced here: 56.7 us
  Pallas kernels  56 us (99%)
  between operations  0.64 us (1%)
    pallas_call x1, Pallas kernels, local(): pl.pallas_call(kernel, out_shape=(pltpu.VMEM((SLICES, ROWS, LANES), F32),...  55.3 us

profile of v5, /device:TPU:1, one launch (start us, length us, event | category | flops | bytes accessed | tf_op | source)
XLA Modules:
  0.0 56.7 jit_solution(6188729980707352802)
XLA Ops:
  0.6 55.3 %adjoint.1 = (f32[2,16,128]{2,1,0:T(8,128)S(1)}, f32[2,2,16,1024]{3,2,1,0:T(8,128)S(1)}) custom-call(s32[2]{0:T(128)} %led_hbm.1, f32[2,2,2,16,1024]{4,3,2,1,0:T(8,128)} %fields_hbm.1, f32[2,16,1024]{2,1,0:T(8,128)} %phases_hbm.1, f32[2,2,16,1024]{3,2,1,0:T(8,128)} %residual_hbm.1, f32[256,256]{1,0:T(8,128)} %constant.10.clone.wide_hbm, ...), custom_call_target="tpu_custom_call" | custom-call | tf_op jit(solution)/shard_map/adjoint/pallas_call | solution.py:472
  55.9 0.7 %emit.1 = (f32[2,16,128]{2,1,0:T(8,128)}, f32[2,2,16,1024]{3,2,1,0:T(8,128)}) custom-call(f32[2,16,128]{2,1,0:T(8,128)S(1)} %get-tuple-element.4.slopes_in, f32[2,2,16,1024]{3,2,1,0:T(8,128)S(1)} %get-tuple-element.5.wave_in), custom_call_target="tpu_custom_call" | custom-call | tf_op jit(solution)/shard_map/emit/pallas_call | solution.py:486

commit v6 on v5

--- a/solution.py
+++ b/solution.py
@@ -125,7 +125,13 @@
     for k in range(8):
         re, im = (real[k], imag[k]) if k == 0 else twist(real[k], imag[k], turn_cos[k], turn_sin[k])
         rows.append(jnp.concatenate([re, im], axis=1))
-    return dot3(wide, split(jnp.concatenate(rows, axis=0)), ((1,), (1,)))
+    waves = split(jnp.concatenate(rows, axis=0))
+    for low in (0, LANES // 2):
+        part = [
+            jnp.concatenate([w[low : low + LANES // 2], w[LANES + low : LANES + low + LANES // 2]], axis=0)
+            for w in wide
+        ]
+        yield dot3(part, waves, ((1,), (1,)))
 
 
 def row_inverse(swapped, turn_cos, turn_sin, wide):
@@ -307,12 +313,18 @@
 
     def to_columns(turn, led):
         seed = wave.at[led]
-        spectrum = row_forward(
+        spectra = row_forward(
             columns_of(seed, 0), columns_of(seed, 1), turn_cos, turn_sin, halves(wide_ref)
         )
-        values = [spectrum[OWNERS * j : OWNERS * (j + 1)] for j in range(2 * PART)]
-        put(values[0:2] + values[4:6], col_out.at[turn, 0, led], OWNERS)
-        put(values[2:4] + values[6:8], col_out.at[turn, 1, led], OWNERS)
+        for half, spectrum in enumerate(spectra):
+            values = [spectrum[OWNERS * j : OWNERS * (j + 1)] for j in range(PART)]
+            put(values, col_out.at[turn, half, led], OWNERS)
+            if half == 0:
+                @pl.when(turn + led == 0)
+                def _():
+                    pl.semaphore_wait(barrier, PEERS - 1 + GROUPS - 1)
+
+            send_columns(turn, led, half)
 
     def column_pass(turn, half):
         tiles = arrived(col_in.at[turn, half], col_recv_sem.at[turn, half], PEERS)
@@ -377,13 +389,6 @@
             @pl.when(phase < SLICES)
             def _():
                 to_columns(phase, led)
-
-                @pl.when(phase + led == 0)
-                def _():
-                    pl.semaphore_wait(barrier, PEERS - 1 + GROUPS - 1)
-
-                for half in range(HALVES):
-                    send_columns(phase, led, half)
 
             @pl.when(phase > 0)
             def _():

time: 56.8 us -> 56.9 us (level)
  no operation moved by 1% of the time
where the time goes in v6:
time: 56.9 us; the launch traced here: 56.8 us
  Pallas kernels  56.1 us (99%)
  between operations  0.64 us (1%)
    pallas_call x1, Pallas kernels, local(): pl.pallas_call(kernel, out_shape=(pltpu.VMEM((SLICES, ROWS, LANES), F32),...  55.4 us

profile of v6, /device:TPU:1, one launch (start us, length us, event | category | flops | bytes accessed | tf_op | source)
XLA Modules:
  0.0 56.8 jit_solution(9969553704025404358)
XLA Ops:
  0.6 55.4 %adjoint.1 = (f32[2,16,128]{2,1,0:T(8,128)S(1)}, f32[2,2,16,1024]{3,2,1,0:T(8,128)S(1)}) custom-call(s32[2]{0:T(128)} %led_hbm.1, f32[2,2,2,16,1024]{4,3,2,1,0:T(8,128)} %fields_hbm.1, f32[2,16,1024]{2,1,0:T(8,128)} %phases_hbm.1, f32[2,2,16,1024]{3,2,1,0:T(8,128)} %residual_hbm.1, f32[256,256]{1,0:T(8,128)} %constant.10.clone.wide_hbm, ...), custom_call_target="tpu_custom_call" | custom-call | tf_op jit(solution)/shard_map/adjoint/pallas_call | solution.py:477
  56.0 0.7 %emit.1 = (f32[2,16,128]{2,1,0:T(8,128)}, f32[2,2,16,1024]{3,2,1,0:T(8,128)}) custom-call(f32[2,16,128]{2,1,0:T(8,128)S(1)} %get-tuple-element.4.slopes_in, f32[2,2,16,1024]{3,2,1,0:T(8,128)S(1)} %get-tuple-element.5.wave_in), custom_call_target="tpu_custom_call" | custom-call | tf_op jit(solution)/shard_map/emit/pallas_call | solution.py:491
